TPU v7x, 32 devices: a whole 2x2x4 slice. The times are simulated.
32 devices in a mesh: gx: 8 (over z, core), gy: 4 (over y, x).
Axes of the slice: x: 2, y: 2, z: 4, core: 2. Of those that a mesh axis runs over, the one named last changes fastest.
Arguments:
- coil_sources: float32 [8, 128, 128, 128], P(None, 'gx', 'gy'), may hold values from -6 to 6
- tissue_labels: int32 [128, 128, 128], P('gx', 'gy'), may hold values from 0 to 5
- class_conductivity: float32 [6], replicated, may hold values from 0.1 to 2
Outputs:
- potential: float32 [8, 128, 128, 128], P(None, 'gx', 'gy')
All inputs are finite; a program needn't handle non-finite values.
Results may differ from a plain program's by a relative error of at most 0.0003.
Values sent between devices are 32-bit elements; how exact they have to be, the bound alone decides.
A program may use at most 192 MiB of HBM per device.

v0:
```python
import jax
import jax.numpy as jnp
from jax import lax
from jax.sharding import PartitionSpec as P

LEVELS = 5
SWEEPS = 2
COARSE_SWEEPS = 16
CLASSES = 6


damping = 0.8


def padded(cells, sides, width):
    for axis, dim in sides:
        count = lax.axis_size(axis)
        ends = count - 1
        head = lax.slice_in_dim(cells, 0, width, axis=dim)
        tail = lax.slice_in_dim(cells, cells.shape[dim] - width, cells.shape[dim], axis=dim)
        cells = jnp.concatenate(
            [
                lax.ppermute(tail, axis, [(i, (i + 1) % count) for i in range(ends)]),
                cells,
                lax.ppermute(head, axis, [((i + 1) % count, i) for i in range(ends)]),
            ],
            axis=dim,
        )
    return cells


def lookup_table(labels, table):
    result = jnp.zeros(labels.shape, jnp.float32)
    for klass in range(CLASSES):
        result = result + jnp.where(labels == klass, table[klass], jnp.float32(0.0))
    return result


def coarsen_cond(cond):
    sx, sy, sz = cond.shape
    return cond.reshape(sx // 2, 2, sy // 2, 2, sz // 2, 2).mean(axis=(1, 3, 5))


def restrict_sum(field):
    rr, sx, sy, sz = field.shape
    return field.reshape(rr, sx // 2, 2, sy // 2, 2, sz // 2, 2).sum(axis=(2, 4, 6))


def prolong_copy(field):
    rr, sx, sy, sz = field.shape
    grown = jnp.broadcast_to(field[:, :, None, :, None, :, None], (rr, sx, 2, sy, 2, sz, 2))
    return grown.reshape(rr, 2 * sx, 2 * sy, 2 * sz)


def face_coeffs(extended):
    centre = extended[1:-1, 1:-1, :]
    zpadded = jnp.pad(centre, ((0, 0), (0, 0), (1, 1)))
    others = [
        extended[2:, 1:-1, :],
        extended[:-2, 1:-1, :],
        extended[1:-1, 2:, :],
        extended[1:-1, :-2, :],
        zpadded[:, :, 2:],
        zpadded[:, :, :-2],
    ]
    coeffs = [
        jnp.where(other > 0, 2.0 * centre * other / (centre + other), centre) for other in others
    ]
    face_sum = coeffs[0] + coeffs[1] + coeffs[2] + coeffs[3] + coeffs[4] + coeffs[5]
    return (coeffs, face_sum)


def apply_operator(extended, field, coeffs, face_sum, scale):
    zpadded = jnp.pad(field, ((0, 0), (0, 0), (0, 0), (1, 1)))
    others = [
        extended[:, 2:, 1:-1, :],
        extended[:, :-2, 1:-1, :],
        extended[:, 1:-1, 2:, :],
        extended[:, 1:-1, :-2, :],
        zpadded[:, :, :, 2:],
        zpadded[:, :, :, :-2],
    ]
    total = coeffs[0] * others[0]
    for index in range(1, 6):
        total = total + coeffs[index] * others[index]
    return scale * (face_sum * field - total)


def field_rim(field):
    return padded(field, (("gx", 1), ("gy", 2)), 1)


def cond_rim(cond):
    return padded(cond, (("gx", 0), ("gy", 1)), 1)


def local_field_pad(field):
    return jnp.pad(field, ((0, 0), (1, 1), (1, 1), (0, 0)))


def local_cond_pad(cond):
    return jnp.pad(cond, ((1, 1), (1, 1), (0, 0)))


def relax(field, source, coeffs, face_sum, scale, count, padder):
    diagonal = scale * face_sum
    for sweep_index in range(count):
        field = (
            field
            + damping
            * (source - apply_operator(padder(field), field, coeffs, face_sum, scale))
            / diagonal
        )
    return field


def local_vcycle(level, source, conductivities, first):
    scale = jnp.float32(2.0**level)
    coeffs, face_sum = face_coeffs(local_cond_pad(conductivities[level - first]))
    diagonal = scale * face_sum
    field = damping * source / diagonal
    return relax(field, source, coeffs, face_sum, scale, COARSE_SWEEPS - 1, local_field_pad)


def local(coil_sources, tissue_labels, class_conductivity):
    depth = LEVELS - 1
    conductivities = [lookup_table(tissue_labels, class_conductivity)]
    for level in range(depth):
        conductivities.append(coarsen_cond(conductivities[-1]))
    stored = []
    source = coil_sources
    for level in range(depth):
        scale = jnp.float32(2.0**level)
        coeffs, face_sum = face_coeffs(cond_rim(conductivities[level]))
        field = damping * source / (scale * face_sum)
        field = relax(field, source, coeffs, face_sum, scale, SWEEPS - 1, field_rim)
        residual = source - apply_operator(field_rim(field), field, coeffs, face_sum, scale)
        stored.append((field, source, coeffs, face_sum, source, scale))
        source = restrict_sum(residual)
    block_x = source.shape[1]
    block_y = source.shape[2]
    gathered, coarse_cond = (
        lax.all_gather(source, "gy", axis=2, tiled=True),
        lax.all_gather(conductivities[depth], "gy", axis=1, tiled=True),
    )
    gathered, coarse_cond = (
        lax.all_gather(gathered, "gx", axis=1, tiled=True),
        lax.all_gather(coarse_cond, "gx", axis=0, tiled=True),
    )
    coarse_list = [coarse_cond]
    correction = local_vcycle(depth, gathered, coarse_list, depth)
    correction = lax.dynamic_slice_in_dim(correction, lax.axis_index("gx") * block_x, block_x, 1)
    correction = lax.dynamic_slice_in_dim(correction, lax.axis_index("gy") * block_y, block_y, 2)
    for level in range(depth - 1, -1, -1):
        field, source, coeffs, face_sum, source_ext, scale = stored[level]
        field = field + prolong_copy(correction)
        correction = relax(field, source, coeffs, face_sum, scale, SWEEPS, field_rim)
    return correction


def solution(mesh):
    in_specs = (P(None, "gx", "gy", None), P("gx", "gy", None), P())
    out_specs = P(None, "gx", "gy", None)
    return jax.shard_map(local, mesh=mesh, in_specs=in_specs, out_specs=out_specs, check_vma=False)
```

profile of v0, /device:TPU:16, one launch (start us, length us, event | category | flops | bytes accessed | tf_op | source)
XLA Modules:
  0.0 563.4 jit_solution(10171521428862776019)
XLA Ops:
  1.5 5.0 select_add_fusion
  8.5 3.6 collective-permute-start
  12.1 18.1 %reshape.94 = f32[8,2,16,2,64,2]{5,4,3,2,1,0:T(8,128)} reshape(f32[16,32,128]{2,1,0:T(8,128)S(1)} %select_add_fusion) | data formatting | bytes 524288 | tf_op jit(solution)/shard_map/reshape | solution.py:41
  30.2 7.0 %reduce_sum.89 = f32[8,16,64]{2,1,0:T(8,128)S(1)} reduce(f32[8,2,16,2,64,2]{5,4,3,2,1,0:T(8,128)} %reshape.94, f32[]{:T(128)} %constant.32.clone.1), dimensions={1,3,5}, to_apply=%region_1.2 | reduce | flops 57344 | bytes 294916 | tf_op jit(solution)/shard_map/reduce_sum | solution.py:41
  39.8 3.6 collective-permute-start.12
  50.3 4.5 collective-permute-start.3
  76.4 4.3 collective-permute-start.7
  83.4 6.3 %collective-permute-start.15 = (f32[10,1,64]{2,1,0:T(1,128)S(1)}, f32[10,1,64]{2,1,0:T(1,128)S(1)}, u32[]{:S(2)}, u32[]{:S(2)}) collective-permute-start(f32[10,1,64]{2,1,0:T(1,128)S(1)} %get-tuple-element.103), channel_id=1, source_target_pairs={{0,1},{1,2},{2,3},{4,5},{5,6},{6,7},{8,9},{9,10},{10,11},{12,13},{... | collective-permute-start | bytes 7688 | tf_op jit(solution)/shard_map/ppermute | solution.py:23
  90.0 4.6 fusion.7
  103.0 4.8 collective-permute-start.11
  110.1 4.0 collective-permute-done.10
  114.2 4.4 fusion.13
  118.6 18.0 %copy.522 = f32[8,16,32,128]{0,3,2,1:T(8,128)} copy(f32[8,16,32,128]{3,2,1,0:T(8,128)} %fusion.13) | data formatting | bytes 4194304 | tf_op jit(solution)/shard_map/sub | solution.py:137
  136.6 24.3 %reduce_sum.88 = f32[8,8,16,64]{0,3,2,1:T(8,128)} reduce(f32[8,8,2,16,2,64,2]{0,6,5,4,3,2,1:T(2,128)} %bitcast.21, f32[]{:T(128)} %constant.32.clone.1), dimensions={2,4,6}, to_apply=%region_0.1 | reduce | flops 458752 | bytes 2359300 | tf_op jit(solution)/shard_map/reduce_sum | solution.py:46
  172.4 4.8 collective-permute-start.19
  180.6 5.2 collective-permute-start.27
  194.1 4.8 collective-permute-start.23
  200.9 3.9 collective-permute-done.22
  208.1 4.8 reduce_sum.90
  219.8 3.7 collective-permute-start.37
  231.9 5.2 collective-permute-start.39
  249.2 5.4 collective-permute-start.35
  261.8 3.8 fusion.76
  274.1 7.1 %all-gather.4 = f32[4,2,8]{2,1,0:T(2,128)S(1)} all-gather(f32[1,2,8]{2,1,0:T(2,128)} %multiply_bitcast_fusion), channel_id=4, replica_groups=mesh['gx'=8,'gy'=4] {'gy'}, dimensions={0}, use_global_device_ids=true | all-gather | bytes 320 | tf_op jit(solution)/shard_map/all_gather | solution.py:144
  281.2 13.3 %all-gather.3 = f32[64,8]{1,0:T(8,128)S(1)} all-gather(f32[8,8]{1,0:T(8,128)S(1)} %bitcast.46), channel_id=5, replica_groups=mesh['gx'=8,'gy'=4] {'gx'}, dimensions={0}, use_global_device_ids=true | all-gather | bytes 2304 | tf_op jit(solution)/shard_map/all_gather | solution.py:148
  300.5 3.8 collective-permute-done.42
  314.1 4.3 collective-permute-start.47
  320.3 3.9 collective-permute-done.46
  328.6 7.7 %all-gather = f32[8,8,8]{2,0,1:T(8,128)S(1)} all-gather(f32[8,2,8]{2,0,1:T(8,128)} %copy.527), channel_id=2, replica_groups=mesh['gx'=8,'gy'=4] {'gy'}, dimensions={1}, use_global_device_ids=true | all-gather | bytes 2560 | tf_op jit(solution)/shard_map/all_gather | solution.py:143
  336.3 13.0 %all-gather.1 = f32[8,64,8]{2,0,1:T(8,128)S(1)} all-gather(f32[8,8,8]{2,0,1:T(8,128)S(1)} %all-gather), channel_id=3, replica_groups=mesh['gx'=8,'gy'=4] {'gx'}, dimensions={1}, use_global_device_ids=true | all-gather | bytes 18432 | tf_op jit(solution)/shard_map/all_gather | solution.py:147
  356.4 4.6 collective-permute-start.48
  370.8 4.2 collective-permute-done.50
  383.5 4.3 collective-permute-start.55
  389.4 4.2 collective-permute-done.54
  399.5 3.8 collective-permute-done.57
  408.3 4.3 collective-permute-done.58
  418.7 3.8 collective-permute-done.61
  427.5 4.3 collective-permute-done.62
  433.4 4.2 broadcast_in_dim.54
  454.5 4.2 collective-permute-done.66
  471.6 4.2 collective-permute-done.70
  480.8 16.0 %broadcast_in_dim.55 = f32[8,8,2,16,2,64,2]{0,6,5,4,3,2,1:T(2,128)} broadcast(f32[8,8,16,64]{0,3,2,1:T(8,128)} %copy.532), dimensions={0,1,3,5} | broadcast | bytes 2359296 | tf_op jit(solution)/shard_map/broadcast_in_dim | solution.py:51
  496.8 20.1 %copy.533 = f32[8,16,32,128]{3,2,1,0:T(8,128)} copy(f32[8,16,32,128]{0,3,2,1:T(8,128)} %bitcast.22) | data formatting | bytes 4194304 | tf_op jit(solution)/shard_map/reshape | solution.py:52
  524.2 3.8 collective-permute-done.73
  533.0 4.2 collective-permute-done.74
  545.4 3.8 collective-permute-done.77
  554.2 4.2 collective-permute-done.78
  558.5 4.5 fusion.31
  (435 shorter events, 250.3 us)
Async XLA Ops:
  6.5 42.4 %collective-permute-start.1 = (f32[1,32,128]{2,1,0:T(8,128)S(1)}, f32[1,32,128]{2,1,0:T(8,128)S(1)}, u32[]{:S(2)}, u32[]{:S(2)}) collective-permute-start(f32[1,32,128]{2,1,0:T(8,128)S(1)} %get-tuple-element.94), channel_id=1, source_target_pairs={{0,4},{4,8},{8,12},{12,16},{16,20},{20,24},{24,28},{1,5},{5,9},{9,... | collective-permute-start | bytes 49160 | tf_op jit(solution)/shard_map/ppermute | solution.py:23
  8.5 40.5 %collective-permute-start = (f32[1,32,128]{2,1,0:T(8,128)S(1)}, f32[1,32,128]{2,1,0:T(8,128)S(1)}, u32[]{:S(2)}, u32[]{:S(2)}) collective-permute-start(f32[1,32,128]{2,1,0:T(8,128)S(1)} %get-tuple-element.93), channel_id=1, source_target_pairs={{4,0},{8,4},{12,8},{16,12},{20,16},{24,20},{28,24},{5,1},{9,5},{13... | collective-permute-start | bytes 49160 | tf_op jit(solution)/shard_map/ppermute | solution.py:25
  37.9 42.8 %collective-permute-start.13 = (f32[1,16,64]{2,1,0:T(8,128)}, f32[1,16,64]{2,1,0:T(8,128)S(1)}, u32[]{:S(2)}, u32[]{:S(2)}) collective-permute-start(f32[1,16,64]{2,1,0:T(8,128)} %get-tuple-element.114), channel_id=1, source_target_pairs={{0,4},{4,8},{8,12},{12,16},{16,20},{20,24},{24,28},{1,5},{5,9},{9,... | collective-permute-start | bytes 12296 | tf_op jit(solution)/shard_map/ppermute | solution.py:23
  39.8 42.2 %collective-permute-start.12 = (f32[1,16,64]{2,1,0:T(8,128)}, f32[1,16,64]{2,1,0:T(8,128)S(1)}, u32[]{:S(2)}, u32[]{:S(2)}) collective-permute-start(f32[1,16,64]{2,1,0:T(8,128)} %get-tuple-element.113), channel_id=1, source_target_pairs={{4,0},{8,4},{12,8},{16,12},{20,16},{24,20},{28,24},{5,1},{9,5},{13... | collective-permute-start | bytes 12296 | tf_op jit(solution)/shard_map/ppermute | solution.py:25
  50.3 5.9 %collective-permute-start.3 = (f32[18,1,128]{2,1,0:T(1,128)S(1)}, f32[18,1,128]{2,1,0:T(1,128)S(1)}, u32[]{:S(2)}, u32[]{:S(2)}) collective-permute-start(f32[18,1,128]{2,1,0:T(1,128)S(1)} %get-tuple-element.91), channel_id=1, source_target_pairs={{0,1},{1,2},{2,3},{4,5},{5,6},{6,7},{8,9},{9,10},{10,11},{12,13},{... | collective-permute-start | bytes 27656 | tf_op jit(solution)/shard_map/ppermute | solution.py:23
  61.8 10.6 %collective-permute-start.4 = (f32[8,1,32,128]{3,2,1,0:T(8,128)}, f32[8,1,32,128]{3,2,1,0:T(8,128)}, u32[]{:S(2)}, u32[]{:S(2)}) collective-permute-start(f32[8,1,32,128]{3,2,1,0:T(8,128)} %get-tuple-element.58), channel_id=1, source_target_pairs={{4,0},{8,4},{12,8},{16,12},{20,16},{24,20},{28,24},{5,1},{9,5},{13... | collective-permute-start | bytes 393224 | tf_op jit(solution)/shard_map/ppermute | solution.py:25
  63.7 11.3 %collective-permute-start.5 = (f32[8,1,32,128]{3,2,1,0:T(8,128)}, f32[8,1,32,128]{3,2,1,0:T(8,128)}, u32[]{:S(2)}, u32[]{:S(2)}) collective-permute-start(f32[8,1,32,128]{3,2,1,0:T(8,128)} %get-tuple-element.57), channel_id=1, source_target_pairs={{0,4},{4,8},{8,12},{12,16},{16,20},{20,24},{24,28},{1,5},{5,9},{9,... | collective-permute-start | bytes 393224 | tf_op jit(solution)/shard_map/ppermute | solution.py:23
  66.7 111.8 %collective-permute-start.25 = (f32[1,8,32]{2,1,0:T(8,128)}, f32[1,8,32]{2,1,0:T(8,128)}, u32[]{:S(2)}, u32[]{:S(2)}) collective-permute-start(f32[1,8,32]{2,1,0:T(8,128)} %get-tuple-element.118), channel_id=1, source_target_pairs={{0,4},{4,8},{8,12},{12,16},{16,20},{20,24},{24,28},{1,5},{5,9},{9,... | collective-permute-start | bytes 3080 | tf_op jit(solution)/shard_map/ppermute | solution.py:23
  72.4 106.1 %collective-permute-start.24 = (f32[1,8,32]{2,1,0:T(8,128)}, f32[1,8,32]{2,1,0:T(8,128)}, u32[]{:S(2)}, u32[]{:S(2)}) collective-permute-start(f32[1,8,32]{2,1,0:T(8,128)} %get-tuple-element.117), channel_id=1, source_target_pairs={{4,0},{8,4},{12,8},{16,12},{20,16},{24,20},{28,24},{5,1},{9,5},{13... | collective-permute-start | bytes 3080 | tf_op jit(solution)/shard_map/ppermute | solution.py:25
  76.4 7.0 %collective-permute-start.7 = (f32[8,18,1,128]{3,0,2,1:T(8,128)S(1)}, f32[8,18,1,128]{3,0,2,1:T(8,128)S(1)}, u32[]{:S(2)}, u32[]{:S(2)}) collective-permute-start(f32[8,18,1,128]{3,0,2,1:T(8,128)S(1)} %copy.516), channel_id=1, source_target_pairs={{0,1},{1,2},{2,3},{4,5},{5,6},{6,7},{8,9},{9,10},{10,11},{12,13},{... | collective-permute-start | bytes 221192 | tf_op jit(solution)/shard_map/ppermute | solution.py:23
  80.7 9.1 %collective-permute-start.6 = (f32[8,18,1,128]{3,0,2,1:T(8,128)S(1)}, f32[8,18,1,128]{3,0,2,1:T(8,128)S(1)}, u32[]{:S(2)}, u32[]{:S(2)}) collective-permute-start(f32[8,18,1,128]{3,0,2,1:T(8,128)S(1)} %copy.514), channel_id=1, source_target_pairs={{1,0},{2,1},{3,2},{5,4},{6,5},{7,6},{9,8},{10,9},{11,10},{13,12},{... | collective-permute-start | bytes 221192 | tf_op jit(solution)/shard_map/ppermute | solution.py:25
  82.1 14.5 %collective-permute-start.14 = (f32[10,1,64]{2,1,0:T(1,128)S(1)}, f32[10,1,64]{2,1,0:T(1,128)S(1)}, u32[]{:S(2)}, u32[]{:S(2)}) collective-permute-start(f32[10,1,64]{2,1,0:T(1,128)S(1)} %get-tuple-element.104), channel_id=1, source_target_pairs={{1,0},{2,1},{3,2},{5,4},{6,5},{7,6},{9,8},{10,9},{11,10},{13,12},{... | collective-permute-start | bytes 7688 | tf_op jit(solution)/shard_map/ppermute | solution.py:25
  83.4 15.6 %collective-permute-start.15 = (f32[10,1,64]{2,1,0:T(1,128)S(1)}, f32[10,1,64]{2,1,0:T(1,128)S(1)}, u32[]{:S(2)}, u32[]{:S(2)}) collective-permute-start(f32[10,1,64]{2,1,0:T(1,128)S(1)} %get-tuple-element.103), channel_id=1, source_target_pairs={{0,1},{1,2},{2,3},{4,5},{5,6},{6,7},{8,9},{9,10},{10,11},{12,13},{... | collective-permute-start | bytes 7688 | tf_op jit(solution)/shard_map/ppermute | solution.py:23
  94.6 5.9 %collective-permute-start.8 = (f32[8,1,32,128]{3,2,1,0:T(8,128)S(1)}, f32[8,1,32,128]{3,2,1,0:T(8,128)S(1)}, u32[]{:S(2)}, u32[]{:S(2)}) collective-permute-start(f32[8,1,32,128]{3,2,1,0:T(8,128)S(1)} %get-tuple-element.56), channel_id=1, source_target_pairs={{4,0},{8,4},{12,8},{16,12},{20,16},{24,20},{28,24},{5,1},{9,5},{13... | collective-permute-start | bytes 393224 | tf_op jit(solution)/shard_map/ppermute | solution.py:25
  96.6 6.3 %collective-permute-start.9 = (f32[8,1,32,128]{3,2,1,0:T(8,128)S(1)}, f32[8,1,32,128]{3,2,1,0:T(8,128)S(1)}, u32[]{:S(2)}, u32[]{:S(2)}) collective-permute-start(f32[8,1,32,128]{3,2,1,0:T(8,128)S(1)} %get-tuple-element.55), channel_id=1, source_target_pairs={{0,4},{4,8},{8,12},{12,16},{16,20},{20,24},{24,28},{1,5},{5,9},{9,... | collective-permute-start | bytes 393224 | tf_op jit(solution)/shard_map/ppermute | solution.py:23
  103.0 7.0 %collective-permute-start.11 = (f32[8,18,1,128]{3,0,2,1:T(8,128)S(1)}, f32[8,18,1,128]{3,0,2,1:T(8,128)S(1)}, u32[]{:S(2)}, u32[]{:S(2)}) collective-permute-start(f32[8,18,1,128]{3,0,2,1:T(8,128)S(1)} %copy.520), channel_id=1, source_target_pairs={{0,1},{1,2},{2,3},{4,5},{5,6},{6,7},{8,9},{9,10},{10,11},{12,13},{... | collective-permute-start | bytes 221192 | tf_op jit(solution)/shard_map/ppermute | solution.py:23
  107.8 6.2 %collective-permute-start.10 = (f32[8,18,1,128]{3,0,2,1:T(8,128)S(1)}, f32[8,18,1,128]{3,0,2,1:T(8,128)S(1)}, u32[]{:S(2)}, u32[]{:S(2)}) collective-permute-start(f32[8,18,1,128]{3,0,2,1:T(8,128)S(1)} %copy.518), channel_id=1, source_target_pairs={{1,0},{2,1},{3,2},{5,4},{6,5},{7,6},{9,8},{10,9},{11,10},{13,12},{... | collective-permute-start | bytes 221192 | tf_op jit(solution)/shard_map/ppermute | solution.py:25
  172.4 13.4 %collective-permute-start.19 = (f32[8,10,1,64]{3,2,1,0:T(1,128)S(1)}, f32[8,10,1,64]{3,2,1,0:T(1,128)S(1)}, u32[]{:S(2)}, u32[]{:S(2)}) collective-permute-start(f32[8,10,1,64]{3,2,1,0:T(1,128)S(1)} %get-tuple-element.74), channel_id=1, source_target_pairs={{0,1},{1,2},{2,3},{4,5},{5,6},{6,7},{8,9},{9,10},{10,11},{12,13},{... | collective-permute-start | bytes 61448 | tf_op jit(solution)/shard_map/ppermute | solution.py:23
  177.2 8.6 %collective-permute-start.18 = (f32[8,10,1,64]{3,2,1,0:T(1,128)S(1)}, f32[8,10,1,64]{3,2,1,0:T(1,128)S(1)}, u32[]{:S(2)}, u32[]{:S(2)}) collective-permute-start(f32[8,10,1,64]{3,2,1,0:T(1,128)S(1)} %get-tuple-element.73), channel_id=1, source_target_pairs={{1,0},{2,1},{3,2},{5,4},{6,5},{7,6},{9,8},{10,9},{11,10},{13,12},{... | collective-permute-start | bytes 61448 | tf_op jit(solution)/shard_map/ppermute | solution.py:25
  179.3 11.6 %collective-permute-start.26 = (f32[6,1,32]{2,1,0:T(1,128)S(1)}, f32[6,1,32]{2,1,0:T(1,128)S(1)}, u32[]{:S(2)}, u32[]{:S(2)}) collective-permute-start(f32[6,1,32]{2,1,0:T(1,128)S(1)} %get-tuple-element.116), channel_id=1, source_target_pairs={{1,0},{2,1},{3,2},{5,4},{6,5},{7,6},{9,8},{10,9},{11,10},{13,12},{... | collective-permute-start | bytes 2312 | tf_op jit(solution)/shard_map/ppermute | solution.py:25
  180.6 10.3 %collective-permute-start.27 = (f32[6,1,32]{2,1,0:T(1,128)S(1)}, f32[6,1,32]{2,1,0:T(1,128)S(1)}, u32[]{:S(2)}, u32[]{:S(2)}) collective-permute-start(f32[6,1,32]{2,1,0:T(1,128)S(1)} %get-tuple-element.115), channel_id=1, source_target_pairs={{0,1},{1,2},{2,3},{4,5},{5,6},{6,7},{8,9},{9,10},{10,11},{12,13},{... | collective-permute-start | bytes 2312 | tf_op jit(solution)/shard_map/ppermute | solution.py:23
  194.1 6.7 %collective-permute-start.23 = (f32[8,10,1,64]{3,2,1,0:T(1,128)S(1)}, f32[8,10,1,64]{3,2,1,0:T(1,128)S(1)}, u32[]{:S(2)}, u32[]{:S(2)}) collective-permute-start(f32[8,10,1,64]{3,2,1,0:T(1,128)S(1)} %get-tuple-element.72), channel_id=1, source_target_pairs={{0,1},{1,2},{2,3},{4,5},{5,6},{6,7},{8,9},{9,10},{10,11},{12,13},{... | collective-permute-start | bytes 61448 | tf_op jit(solution)/shard_map/ppermute | solution.py:23
  198.9 5.9 %collective-permute-start.22 = (f32[8,10,1,64]{3,2,1,0:T(1,128)S(1)}, f32[8,10,1,64]{3,2,1,0:T(1,128)S(1)}, u32[]{:S(2)}, u32[]{:S(2)}) collective-permute-start(f32[8,10,1,64]{3,2,1,0:T(1,128)S(1)} %get-tuple-element.71), channel_id=1, source_target_pairs={{1,0},{2,1},{3,2},{5,4},{6,5},{7,6},{9,8},{10,9},{11,10},{13,12},{... | collective-permute-start | bytes 61448 | tf_op jit(solution)/shard_map/ppermute | solution.py:25
  214.8 10.6 %collective-permute-start.28 = (f32[8,1,8,32]{0,3,2,1:T(8,128)}, f32[8,1,8,32]{0,3,2,1:T(8,128)}, u32[]{:S(2)}, u32[]{:S(2)}) collective-permute-start(f32[8,1,8,32]{0,3,2,1:T(8,128)} %get-tuple-element.86), channel_id=1, source_target_pairs={{4,0},{8,4},{12,8},{16,12},{20,16},{24,20},{28,24},{5,1},{9,5},{13... | collective-permute-start | bytes 24584 | tf_op jit(solution)/shard_map/ppermute | solution.py:25
  216.7 8.7 %collective-permute-start.29 = (f32[8,1,8,32]{0,3,2,1:T(8,128)}, f32[8,1,8,32]{0,3,2,1:T(8,128)}, u32[]{:S(2)}, u32[]{:S(2)}) collective-permute-start(f32[8,1,8,32]{0,3,2,1:T(8,128)} %get-tuple-element.85), channel_id=1, source_target_pairs={{0,4},{4,8},{8,12},{12,16},{16,20},{20,24},{24,28},{1,5},{5,9},{9,... | collective-permute-start | bytes 24584 | tf_op jit(solution)/shard_map/ppermute | solution.py:23
  219.8 10.8 %collective-permute-start.37 = (f32[1,4,16]{2,1,0:T(4,128)}, f32[1,4,16]{2,1,0:T(4,128)S(1)}, u32[]{:S(2)}, u32[]{:S(2)}) collective-permute-start(f32[1,4,16]{2,1,0:T(4,128)} %get-tuple-element.123), channel_id=1, source_target_pairs={{0,4},{4,8},{8,12},{12,16},{16,20},{20,24},{24,28},{1,5},{5,9},{9,... | collective-permute-start | bytes 776 | tf_op jit(solution)/shard_map/ppermute | solution.py:23
  223.5 7.0 %collective-permute-start.36 = (f32[1,4,16]{2,1,0:T(4,128)}, f32[1,4,16]{2,1,0:T(4,128)S(1)}, u32[]{:S(2)}, u32[]{:S(2)}) collective-permute-start(f32[1,4,16]{2,1,0:T(4,128)} %get-tuple-element.122), channel_id=1, source_target_pairs={{4,0},{8,4},{12,8},{16,12},{20,16},{24,20},{28,24},{5,1},{9,5},{13... | collective-permute-start | bytes 776 | tf_op jit(solution)/shard_map/ppermute | solution.py:25
  226.4 10.7 %collective-permute-start.31 = (f32[8,6,1,32]{0,3,2,1:T(8,128)S(1)}, f32[8,6,1,32]{0,3,2,1:T(8,128)S(1)}, u32[]{:S(2)}, u32[]{:S(2)}) collective-permute-start(f32[8,6,1,32]{0,3,2,1:T(8,128)S(1)} %get-tuple-element.66), channel_id=1, source_target_pairs={{0,1},{1,2},{2,3},{4,5},{5,6},{6,7},{8,9},{9,10},{10,11},{12,13},{... | collective-permute-start | bytes 18440 | tf_op jit(solution)/shard_map/ppermute | solution.py:23
  229.2 7.9 %collective-permute-start.30 = (f32[8,6,1,32]{0,3,2,1:T(8,128)S(1)}, f32[8,6,1,32]{0,3,2,1:T(8,128)S(1)}, u32[]{:S(2)}, u32[]{:S(2)}) collective-permute-start(f32[8,6,1,32]{0,3,2,1:T(8,128)S(1)} %get-tuple-element.65), channel_id=1, source_target_pairs={{1,0},{2,1},{3,2},{5,4},{6,5},{7,6},{9,8},{10,9},{11,10},{13,12},{... | collective-permute-start | bytes 18440 | tf_op jit(solution)/shard_map/ppermute | solution.py:25
  230.6 14.0 %collective-permute-start.38 = (f32[4,1,16]{2,1,0:T(1,128)S(1)}, f32[4,1,16]{2,1,0:T(1,128)S(1)}, u32[]{:S(2)}, u32[]{:S(2)}) collective-permute-start(f32[4,1,16]{2,1,0:T(1,128)S(1)} %get-tuple-element.120), channel_id=1, source_target_pairs={{1,0},{2,1},{3,2},{5,4},{6,5},{7,6},{9,8},{10,9},{11,10},{13,12},{... | collective-permute-start | bytes 776 | tf_op jit(solution)/shard_map/ppermute | solution.py:25
  231.9 12.7 %collective-permute-start.39 = (f32[4,1,16]{2,1,0:T(1,128)S(1)}, f32[4,1,16]{2,1,0:T(1,128)S(1)}, u32[]{:S(2)}, u32[]{:S(2)}) collective-permute-start(f32[4,1,16]{2,1,0:T(1,128)S(1)} %get-tuple-element.119), channel_id=1, source_target_pairs={{0,1},{1,2},{2,3},{4,5},{5,6},{6,7},{8,9},{9,10},{10,11},{12,13},{... | collective-permute-start | bytes 776 | tf_op jit(solution)/shard_map/ppermute | solution.py:23
  240.2 6.4 %collective-permute-start.32 = (f32[8,1,8,32]{0,3,2,1:T(8,128)S(1)}, f32[8,1,8,32]{0,3,2,1:T(8,128)S(1)}, u32[]{:S(2)}, u32[]{:S(2)}) collective-permute-start(f32[8,1,8,32]{0,3,2,1:T(8,128)S(1)} %get-tuple-element.84), channel_id=1, source_target_pairs={{4,0},{8,4},{12,8},{16,12},{20,16},{24,20},{28,24},{5,1},{9,5},{13... | collective-permute-start | bytes 24584 | tf_op jit(solution)/shard_map/ppermute | solution.py:25
  242.2 6.3 %collective-permute-start.33 = (f32[8,1,8,32]{0,3,2,1:T(8,128)S(1)}, f32[8,1,8,32]{0,3,2,1:T(8,128)S(1)}, u32[]{:S(2)}, u32[]{:S(2)}) collective-permute-start(f32[8,1,8,32]{0,3,2,1:T(8,128)S(1)} %get-tuple-element.83), channel_id=1, source_target_pairs={{0,4},{4,8},{8,12},{12,16},{16,20},{20,24},{24,28},{1,5},{5,9},{9,... | collective-permute-start | bytes 24584 | tf_op jit(solution)/shard_map/ppermute | solution.py:23
  249.2 10.3 %collective-permute-start.35 = (f32[8,6,1,32]{0,3,2,1:T(8,128)}, f32[8,6,1,32]{0,3,2,1:T(8,128)}, u32[]{:S(2)}, u32[]{:S(2)}) collective-permute-start(f32[8,6,1,32]{0,3,2,1:T(8,128)} %get-tuple-element.64), channel_id=1, source_target_pairs={{0,1},{1,2},{2,3},{4,5},{5,6},{6,7},{8,9},{9,10},{10,11},{12,13},{... | collective-permute-start | bytes 18440 | tf_op jit(solution)/shard_map/ppermute | solution.py:23
  254.6 7.2 %collective-permute-start.34 = (f32[8,6,1,32]{0,3,2,1:T(8,128)}, f32[8,6,1,32]{0,3,2,1:T(8,128)}, u32[]{:S(2)}, u32[]{:S(2)}) collective-permute-start(f32[8,6,1,32]{0,3,2,1:T(8,128)} %get-tuple-element.63), channel_id=1, source_target_pairs={{1,0},{2,1},{3,2},{5,4},{6,5},{7,6},{9,8},{10,9},{11,10},{13,12},{... | collective-permute-start | bytes 18440 | tf_op jit(solution)/shard_map/ppermute | solution.py:25
  268.5 26.0 %collective-permute-start.40 = (f32[8,1,4,16]{0,3,2,1:T(8,128)}, f32[8,1,4,16]{0,3,2,1:T(8,128)}, u32[]{:S(2)}, u32[]{:S(2)}) collective-permute-start(f32[8,1,4,16]{0,3,2,1:T(8,128)} %get-tuple-element.112), channel_id=1, source_target_pairs={{4,0},{8,4},{12,8},{16,12},{20,16},{24,20},{28,24},{5,1},{9,5},{13... | collective-permute-start | bytes 6152 | tf_op jit(solution)/shard_map/ppermute | solution.py:25
  270.4 24.1 %collective-permute-start.41 = (f32[8,1,4,16]{0,3,2,1:T(8,128)}, f32[8,1,4,16]{0,3,2,1:T(8,128)}, u32[]{:S(2)}, u32[]{:S(2)}) collective-permute-start(f32[8,1,4,16]{0,3,2,1:T(8,128)} %get-tuple-element.111), channel_id=1, source_target_pairs={{0,4},{4,8},{8,12},{12,16},{16,20},{20,24},{24,28},{1,5},{5,9},{9,... | collective-permute-start | bytes 6152 | tf_op jit(solution)/shard_map/ppermute | solution.py:23
  314.1 6.2 %collective-permute-start.47 = (f32[8,4,1,16]{0,3,2,1:T(8,128)S(1)}, f32[8,4,1,16]{0,3,2,1:T(8,128)S(1)}, u32[]{:S(2)}, u32[]{:S(2)}) collective-permute-start(f32[8,4,1,16]{0,3,2,1:T(8,128)S(1)} %get-tuple-element.100), channel_id=1, source_target_pairs={{0,1},{1,2},{2,3},{4,5},{5,6},{6,7},{8,9},{9,10},{10,11},{12,13},{... | collective-permute-start | bytes 6152 | tf_op jit(solution)/shard_map/ppermute | solution.py:23
  356.4 6.5 %collective-permute-start.48 = (f32[8,1,4,16]{0,3,2,1:T(8,128)S(1)}, f32[8,1,4,16]{0,3,2,1:T(8,128)S(1)}, u32[]{:S(2)}, u32[]{:S(2)}) collective-permute-start(f32[8,1,4,16]{0,3,2,1:T(8,128)S(1)} %get-tuple-element.108), channel_id=1, source_target_pairs={{4,0},{8,4},{12,8},{16,12},{20,16},{24,20},{28,24},{5,1},{9,5},{13... | collective-permute-start | bytes 6152 | tf_op jit(solution)/shard_map/ppermute | solution.py:25
  397.0 6.3 %collective-permute-start.57 = (f32[8,1,8,32]{0,3,2,1:T(8,128)S(1)}, f32[8,1,8,32]{0,3,2,1:T(8,128)S(1)}, u32[]{:S(2)}, u32[]{:S(2)}) collective-permute-start(f32[8,1,8,32]{0,3,2,1:T(8,128)S(1)} %get-tuple-element.81), channel_id=1, source_target_pairs={{0,4},{4,8},{8,12},{12,16},{16,20},{20,24},{24,28},{1,5},{5,9},{9,... | collective-permute-start | bytes 24584 | tf_op jit(solution)/shard_map/ppermute | solution.py:23
  406.1 6.5 %collective-permute-start.58 = (f32[8,6,1,32]{0,3,2,1:T(8,128)S(1)}, f32[8,6,1,32]{0,3,2,1:T(8,128)S(1)}, u32[]{:S(2)}, u32[]{:S(2)}) collective-permute-start(f32[8,6,1,32]{0,3,2,1:T(8,128)S(1)} %get-tuple-element.61), channel_id=1, source_target_pairs={{1,0},{2,1},{3,2},{5,4},{6,5},{7,6},{9,8},{10,9},{11,10},{13,12},{... | collective-permute-start | bytes 18440 | tf_op jit(solution)/shard_map/ppermute | solution.py:25
  416.2 6.3 %collective-permute-start.61 = (f32[8,1,8,32]{0,3,2,1:T(8,128)S(1)}, f32[8,1,8,32]{0,3,2,1:T(8,128)S(1)}, u32[]{:S(2)}, u32[]{:S(2)}) collective-permute-start(f32[8,1,8,32]{0,3,2,1:T(8,128)S(1)} %get-tuple-element.79), channel_id=1, source_target_pairs={{0,4},{4,8},{8,12},{12,16},{16,20},{20,24},{24,28},{1,5},{5,9},{9,... | collective-permute-start | bytes 24584 | tf_op jit(solution)/shard_map/ppermute | solution.py:23
  425.3 6.5 %collective-permute-start.62 = (f32[8,6,1,32]{0,3,2,1:T(8,128)S(1)}, f32[8,6,1,32]{0,3,2,1:T(8,128)S(1)}, u32[]{:S(2)}, u32[]{:S(2)}) collective-permute-start(f32[8,6,1,32]{0,3,2,1:T(8,128)S(1)} %get-tuple-element.59), channel_id=1, source_target_pairs={{1,0},{2,1},{3,2},{5,4},{6,5},{7,6},{9,8},{10,9},{11,10},{13,12},{... | collective-permute-start | bytes 18440 | tf_op jit(solution)/shard_map/ppermute | solution.py:25
  469.9 5.9 %collective-permute-start.70 = (f32[8,10,1,64]{3,2,1,0:T(1,128)S(1)}, f32[8,10,1,64]{3,2,1,0:T(1,128)S(1)}, u32[]{:S(2)}, u32[]{:S(2)}) collective-permute-start(f32[8,10,1,64]{3,2,1,0:T(1,128)S(1)} %get-tuple-element.67), channel_id=1, source_target_pairs={{1,0},{2,1},{3,2},{5,4},{6,5},{7,6},{9,8},{10,9},{11,10},{13,12},{... | collective-permute-start | bytes 61448 | tf_op jit(solution)/shard_map/ppermute | solution.py:25
  521.7 6.3 %collective-permute-start.73 = (f32[8,1,32,128]{3,2,1,0:T(8,128)S(1)}, f32[8,1,32,128]{3,2,1,0:T(8,128)S(1)}, u32[]{:S(2)}, u32[]{:S(2)}) collective-permute-start(f32[8,1,32,128]{3,2,1,0:T(8,128)S(1)} %get-tuple-element.53), channel_id=1, source_target_pairs={{0,4},{4,8},{8,12},{12,16},{16,20},{20,24},{24,28},{1,5},{5,9},{9,... | collective-permute-start | bytes 393224 | tf_op jit(solution)/shard_map/ppermute | solution.py:23
  531.0 6.2 %collective-permute-start.74 = (f32[8,18,1,128]{3,0,2,1:T(8,128)S(1)}, f32[8,18,1,128]{3,0,2,1:T(8,128)S(1)}, u32[]{:S(2)}, u32[]{:S(2)}) collective-permute-start(f32[8,18,1,128]{3,0,2,1:T(8,128)S(1)} %copy.534), channel_id=1, source_target_pairs={{1,0},{2,1},{3,2},{5,4},{6,5},{7,6},{9,8},{10,9},{11,10},{13,12},{... | collective-permute-start | bytes 221192 | tf_op jit(solution)/shard_map/ppermute | solution.py:25
  542.9 6.3 %collective-permute-start.77 = (f32[8,1,32,128]{3,2,1,0:T(8,128)S(1)}, f32[8,1,32,128]{3,2,1,0:T(8,128)S(1)}, u32[]{:S(2)}, u32[]{:S(2)}) collective-permute-start(f32[8,1,32,128]{3,2,1,0:T(8,128)S(1)} %get-tuple-element.51), channel_id=1, source_target_pairs={{0,4},{4,8},{8,12},{12,16},{16,20},{20,24},{24,28},{1,5},{5,9},{9,... | collective-permute-start | bytes 393224 | tf_op jit(solution)/shard_map/ppermute | solution.py:23
  552.2 6.2 %collective-permute-start.78 = (f32[8,18,1,128]{3,0,2,1:T(8,128)S(1)}, f32[8,18,1,128]{3,0,2,1:T(8,128)S(1)}, u32[]{:S(2)}, u32[]{:S(2)}) collective-permute-start(f32[8,18,1,128]{3,0,2,1:T(8,128)S(1)} %copy.538), channel_id=1, source_target_pairs={{1,0},{2,1},{3,2},{5,4},{6,5},{7,6},{9,8},{10,9},{11,10},{13,12},{... | collective-permute-start | bytes 221192 | tf_op jit(solution)/shard_map/ppermute | solution.py:25
  (123 other events, 2276.5 us)
where the time goes:
time: 574 us; the launch traced here: 563 us
  starting transfers between devices  201 us (35%)
  other arithmetic  116 us (20%)
  local copies, waits for them, and re-layouts  106 us (18%)
  waiting for transfers between devices  96.5 us (17%)
  blocking collectives  41.1 us (7%)
    ppermute x40, starting transfers between devices, padded(): lax.ppermute(tail, axis, [(i, (i + 1) % count) for i in range(ends)])  128 us
    ppermute x40, starting transfers between devices, padded(): lax.ppermute(head, axis, [((i + 1) % count, i) for i in range(ends)])  73 us
    ppermute x40, waiting for transfers between devices, padded(): lax.ppermute(head, axis, [((i + 1) % count, i) for i in range(ends)])  52.4 us
    ppermute x40, waiting for transfers between devices, padded(): lax.ppermute(tail, axis, [(i, (i + 1) % count) for i in range(ends)])  44 us
    reduce_sum x5, other arithmetic, restrict_sum(): field.reshape(rr, sx // 2, 2, sy // 2, 2, sz // 2, 2).sum(axis=(2, 4, 6))  33.5 us
    add x25, other arithmetic, relax(): field + damping * (source - apply_operator(padder(field), field, coeffs,...  30.3 us
    reshape x2, local copies, waits for them, and re-layouts, prolong_copy(): return grown.reshape(rr, 2 * sx, 2 * sy, 2 * sz)  23.7 us
    sub x2, local copies, waits for them, and re-layouts, local(): source - apply_operator(field_rim(field), field, coeffs, face_sum, scale)  20.7 us
  transfers between devices with their start and end apart: 80, of which 39 were waited for; matrix products, arithmetic and copies ran while one was open for 20% of the time, Pallas kernels for 0%

commit v1 on v0

v1 whole, which is shorter than its diff:
```python
import functools

import jax
import jax.numpy as jnp
from jax import lax
from jax.experimental import pallas as pl
from jax.experimental.pallas import tpu as pltpu
from jax.sharding import PartitionSpec as P

CLASSES = 6
SWEEPS_COARSE = 16
DAMP = 0.8
KEEP = 1.0 - DAMP
MESH = pl.DeviceIdType.MESH
DIRS = [(dx, dy) for dx in (-1, 0, 1) for dy in (-1, 0, 1) if (dx, dy) != (0, 0)]
ROWS = 8


def iota(shape, dim):
    return lax.broadcasted_iota(jnp.int32, shape, dim)


def roll(t, shift, axis):
    return pltpu.roll(t, shift % t.shape[axis], axis)


def pairsum(t, step, axis):
    even = (iota(t.shape, axis) // step) % 2 == 0
    return t + jnp.where(even, roll(t, -step, axis), roll(t, step, axis))


def harmonic(a, b):
    return 2.0 * a * b / (a + b)


class Level:
    def __init__(self, index, bx, by, nz, halo, chalo):
        self.bx, self.by, self.nz = bx, by, nz
        self.h, self.hc, self.step = halo, chalo, 2**index
        self.vshape = (bx + 2 * halo, by + 2 * halo, 8, nz)
        self.cshape = (bx + 2 * chalo, by + 2 * ROWS, nz)


def exchange(src, dst, offs, dims, widths, sems, axes, src_offs=None):
    me, count = axes
    src_offs = offs if src_offs is None else src_offs
    copies = []
    for d, step in enumerate(DIRS):
        s_idx, d_idx = [], []
        for k in (0, 1):
            so, o, n, w = src_offs[k], offs[k], dims[k], widths[k]
            if step[k] == 0:
                s_idx.append(pl.ds(so, n))
                d_idx.append(pl.ds(o, n))
            elif step[k] < 0:
                s_idx.append(pl.ds(so, w))
                d_idx.append(pl.ds(o + n, w))
            else:
                s_idx.append(pl.ds(so + n - w, w))
                d_idx.append(pl.ds(o - w, w))
        target = tuple(lax.rem(me[k] + step[k] + count[k], count[k]) for k in (0, 1))
        copies.append(
            pltpu.make_async_remote_copy(
                src_ref=src.at[tuple(s_idx)],
                dst_ref=dst.at[tuple(d_idx)],
                send_sem=sems.at[0, d],
                recv_sem=sems.at[1, d],
                device_id=target,
                device_id_type=MESH,
            )
        )
    for copy in copies:
        copy.start()
    return copies


def finish(copies):
    for copy in copies:
        copy.wait()


def coefficients(lev, c, kx, ky, kz, kk, ww, me, count):
    rows = lev.cshape[1]
    shape = (rows, lev.nz)
    ycell = iota(shape, 0) - ROWS + me[1] * lev.by
    ylast = count[1] * lev.by - 1
    zlane = iota(shape, 1)
    zfirst, zlast = zlane < lev.step, zlane >= lev.nz - lev.step
    xlast = count[0] * lev.bx - 1
    xbase = me[0] * lev.bx - lev.hc

    def faces(x, carry):
        cc = c[x]
        cell = x + xbase
        xk = jnp.where(jnp.logical_or(cell == 0, cell == xlast + 1), 0.0, harmonic(cc, c[x - 1]))
        kx[x] = xk
        ky[x] = jnp.where(
            jnp.logical_or(ycell == 0, ycell == ylast + 1), 0.0, harmonic(cc, roll(cc, 1, 0))
        )
        kz[x] = jnp.where(zlast, 0.0, harmonic(cc, roll(cc, -lev.step, 1)))
        return carry

    lax.fori_loop(1, lev.cshape[0], faces, 0)

    def sums(x, carry):
        cc = c[x]
        cell = x + xbase
        yk, zk = ky[x], kz[x]
        total = jnp.where(cell == 0, cc, kx[x]) + jnp.where(cell == xlast, cc, kx[x + 1])
        total = total + jnp.where(ycell == 0, cc, yk) + jnp.where(ycell == ylast, cc, roll(yk, -1, 0))
        total = total + jnp.where(zlast, cc, zk) + jnp.where(zfirst, cc, roll(zk, lev.step, 1))
        kk[x] = total
        ww[x] = DAMP / total
        return carry

    lax.fori_loop(1, lev.cshape[0] - 1, sums, 0)


def row_pass(lev, co, v, x, ys, emit):
    kx, ky, kz, kk, ww = co
    xc = x + lev.hc - lev.h
    held, faces = {}, {}

    def value(y):
        if y not in held:
            held[y] = v[x, y]
        return held[y]

    def at(ref, xx, y):
        yy = y + ROWS - lev.h
        return ref[xx, yy : yy + 1, :]

    def yface(y):
        if y not in faces:
            faces[y] = at(ky, xc, y)
        return faces[y]

    for y in ys:
        here = value(y)
        zk = at(kz, xc, y)
        total = at(kx, xc, y) * v[x - 1, y] + at(kx, xc + 1, y) * v[x + 1, y]
        total = total + yface(y) * value(y - 1) + yface(y + 1) * value(y + 1)
        total = total + zk * roll(here, -lev.step, 1) + roll(zk * here, lev.step, 1)
        emit(y, here, total, functools.partial(at, xx=xc, y=y))


def spans(lev, width):
    lo = lev.h - width
    return (lo, lev.h + lev.bx + width), range(lo, lev.h + lev.by + width)


def first_sweep(lev, co, g, out, width):
    (x0, x1), ys = spans(lev, width)

    def body(x, carry):
        xc = x + lev.hc - lev.h
        for y in ys:
            yy = y + ROWS - lev.h
            out[x, y] = co[4][xc, yy : yy + 1, :] * g[x, y]
        return carry

    lax.fori_loop(x0, x1, body, 0)


def sweep(lev, co, g, v, out, width, shift=0):
    (x0, x1), ys = spans(lev, width)

    def body(x, carry):
        def emit(y, here, total, at):
            out[x - shift, y - shift] = KEEP * here + at(co[4]) * (g[x, y] + total)

        row_pass(lev, co, v, x, ys, emit)
        return carry

    lax.fori_loop(x0, x1, body, 0)


def restrict_rows(lev, co, g, v, pair):
    sums = {}
    for dx in (0, 1):
        x = lev.h + 2 * pair + dx

        def emit(y, here, total, at):
            r = g[x, y] + total - at(co[3]) * here
            key = (y - lev.h) // 2
            sums[key] = sums[key] + r if key in sums else r

        row_pass(lev, co, v, x, range(lev.h, lev.h + lev.by), emit)
    return {key: pairsum(t, lev.step, 1) for key, t in sums.items()}


def add_correction(lev, v, corr, out):
    def body(pair, carry):
        for dx in (0, 1):
            x = lev.h + 2 * pair + dx
            for y in range(lev.by):
                out[x, lev.h + y] = v[x, lev.h + y] + corr[pair, y // 2]
        return carry

    lax.fori_loop(0, lev.bx // 2, body, 0)


def coarsen(src, off, bx, by, step, store):
    for x in range(bx // 2):
        t = None
        for dx in (0, 1):
            for dy in (0, 1):
                part = src[off + 2 * x + dx, pl.ds(ROWS + dy, by // 2, stride=2), :]
                t = part if t is None else t + part
        store(x, pairsum(t, step, 1) * 0.25)


class Whole:
    def __init__(self, c, ystep, zstep):
        nx, ny, nl = c.shape
        xi, yi, zi = (iota(c.shape, k) for k in range(3))
        self.ystep, self.zstep = ystep, zstep
        nxt = jnp.concatenate([c[1:], c[-1:]], axis=0)
        self.kx = jnp.where(xi < nx - 1, harmonic(c, nxt), 0.0)
        self.ky = jnp.where(yi < ny - ystep, harmonic(c, roll(c, -ystep, 1)), 0.0)
        self.kz = jnp.where(zi < nl - zstep, harmonic(c, roll(c, -zstep, 2)), 0.0)
        total = jnp.where(xi == nx - 1, c, self.kx) + jnp.where(xi == 0, c, self.back(self.kx))
        total = total + jnp.where(yi >= ny - ystep, c, self.ky)
        total = total + jnp.where(yi < ystep, c, roll(self.ky, ystep, 1))
        total = total + jnp.where(zi >= nl - zstep, c, self.kz)
        total = total + jnp.where(zi < zstep, c, roll(self.kz, zstep, 2))
        self.kk = total
        self.ww = DAMP / total

    def back(self, t):
        return jnp.concatenate([jnp.zeros_like(t[:1]), t[:-1]], axis=0)

    def sums(self, v):
        nxt = jnp.concatenate([v[1:], v[-1:]], axis=0)
        total = self.kx * nxt + self.back(self.kx * v)
        total = total + self.ky * roll(v, -self.ystep, 1) + roll(self.ky * v, self.ystep, 1)
        return total + self.kz * roll(v, -self.zstep, 2) + roll(self.kz * v, self.zstep, 2)

    def sweep(self, v, g):
        return KEEP * v + self.ww * (g + self.sums(v))


def halve(t, zstep):
    nx, ny, nl = t.shape
    t = t.reshape(nx // 2, 2, ny, nl)
    t = t[:, 0] + t[:, 1]
    return pairsum(pairsum(t, 1, 1), zstep, 2)


def double(t):
    nx, ny, nl = t.shape
    return jnp.broadcast_to(t[:, None], (nx, 2, ny, nl)).reshape(2 * nx, ny, nl)


def gather_line(buf, axis, me, count, sems):
    copies = []
    for d in range(1, count[axis]):
        peer = lax.rem(me[axis] + d, count[axis])
        target = (peer, me[1]) if axis == 0 else (me[0], peer)
        piece = buf.at[me[0]] if axis == 0 else buf.at[me[0], me[1]]
        copies.append(
            pltpu.make_async_remote_copy(
                src_ref=piece,
                dst_ref=piece,
                send_sem=sems.at[0, d],
                recv_sem=sems.at[1, d],
                device_id=target,
                device_id_type=MESH,
            )
        )
    for copy in copies:
        copy.start()
    return copies


def finish_line(buf, axis, me, count, sems):
    for d in range(1, count[axis]):
        peer = lax.rem(me[axis] - d + count[axis], count[axis])
        other = lax.rem(me[axis] + d, count[axis])
        target = (other, me[1]) if axis == 0 else (me[0], other)
        mine = buf.at[me[0]] if axis == 0 else buf.at[me[0], me[1]]
        piece = buf.at[peer] if axis == 0 else buf.at[me[0], peer]
        args = dict(
            send_sem=sems.at[0, d], recv_sem=sems.at[1, d], device_id=target, device_id_type=MESH
        )
        pltpu.make_async_remote_copy(src_ref=mine, dst_ref=mine, **args).wait_send()
        pltpu.make_async_remote_copy(src_ref=piece, dst_ref=piece, **args).wait_recv()


def kernel(count, levels, refs_of, table, g_in, labels, out, *scratch):
    r = refs_of(scratch)
    me = (lax.axis_index("gx"), lax.axis_index("gy"))
    axes = (me, count)
    l0, l1, l2 = levels
    bx3, by3 = l2.bx // 2, l2.by // 2

    barrier = pltpu.get_barrier_semaphore()
    greeted = [(d, 0) for d in range(1, count[0])] + [(0, d) for d in range(1, count[1])]
    greeted += [(dx % count[0], dy % count[1]) for dx, dy in DIRS if dx and dy]
    for dx, dy in greeted:
        target = (lax.rem(me[0] + dx, count[0]), lax.rem(me[1] + dy, count[1]))
        pl.semaphore_signal(barrier, inc=1, device_id=target, device_id_type=MESH)

    fetch = pltpu.make_async_copy(
        g_in, r["g0"].at[pl.ds(l0.h, l0.bx), pl.ds(l0.h, l0.by)], r["local"]
    )
    fetch.start()

    c0, c1, c2 = r["c0"], r["c1"], r["c2"]

    def look_up(x, carry):
        lab = labels[x]
        t = jnp.zeros(lab.shape, jnp.float32)
        for klass in range(CLASSES):
            t = jnp.where(lab == klass, table[klass], t)
        c0[l0.hc + x, ROWS : ROWS + l0.by, :] = t
        return carry

    lax.fori_loop(0, l0.bx, look_up, 0)

    def put1(x, t):
        c1[l1.hc + x, ROWS : ROWS + l1.by, :] = t

    def put2(x, t):
        c2[l2.hc + x, ROWS : ROWS + l2.by, :] = t

    def put3(x, t):
        r["c3"][me[0], me[1], x * by3 : (x + 1) * by3, :] = t

    pl.semaphore_wait(barrier, len(greeted))
    e = r["ex"]
    exg0 = exchange(
        g_in, r["g0"], (l0.h,) * 2, (l0.bx, l0.by), (l0.h,) * 2, e.at[0], axes, src_offs=(0, 0)
    )

    def cond_exchange(lev, c, k):
        return exchange(
            c, c, (lev.hc, ROWS), (lev.bx, lev.by), (lev.hc, ROWS), e.at[k], axes
        )

    exc0 = cond_exchange(l0, c0, 1)
    coarsen(c0, l0.hc, l0.bx, l0.by, 1, put1)
    exc1 = cond_exchange(l1, c1, 2)
    coarsen(c1, l1.hc, l1.bx, l1.by, 2, put2)
    exc2 = cond_exchange(l2, c2, 3)
    coarsen(c2, l2.hc, l2.bx, l2.by, 4, put3)
    gather_line(r["c3"], 1, me, count, r["gat"].at[0])

    finish(exc0)
    co0 = [r[n + "0"] for n in ("kx", "ky", "kz", "kk", "ww")]
    co1 = [r[n + "1"] for n in ("kx", "ky", "kz", "kk", "ww")]
    co2 = [r[n + "2"] for n in ("kx", "ky", "kz", "kk", "ww")]
    coefficients(l0, c0, *co0, me, count)
    fetch.wait()
    finish(exg0)

    first_sweep(l0, co0, r["g0"], r["a0"], 2)
    sweep(l0, co0, r["g0"], r["a0"], r["b0"], 1)

    def down(lev, co, g, v, nxt, gn):
        def body(pair, carry):
            for key, t in restrict_rows(lev, co, g, v, pair).items():
                gn[nxt.h + pair, nxt.h + key] = t
            return carry

        lax.fori_loop(0, nxt.bx, body, 0)

    down(l0, co0, r["g0"], r["b0"], l1, r["g1"])

    def field_exchange(lev, f, k):
        return exchange(f, f, (lev.h,) * 2, (lev.bx, lev.by), (lev.h,) * 2, e.at[k], axes)

    exg1 = field_exchange(l1, r["g1"], 4)
    finish_line(r["c3"], 1, me, count, r["gat"].at[0])
    gather_line(r["c3"], 0, me, count, r["gat"].at[1])
    finish(exc1)
    finish(exc2)
    coefficients(l1, c1, *co1, me, count)
    finish(exg1)
    first_sweep(l1, co1, r["g1"], r["a1"], 2)
    sweep(l1, co1, r["g1"], r["a1"], r["b1"], 1)
    down(l1, co1, r["g1"], r["b1"], l2, r["g2"])

    exg2 = field_exchange(l2, r["g2"], 5)
    coefficients(l2, c2, *co2, me, count)
    finish(exg2)
    first_sweep(l2, co2, r["g2"], r["a2"], 3)
    sweep(l2, co2, r["g2"], r["a2"], r["b2"], 2)
    lane8 = iota((8, l2.nz), 1) % 8
    sub8 = iota((8, l2.nz), 0)
    for pair in range(bx3):
        for key, t in restrict_rows(l2, co2, r["g2"], r["b2"], pair).items():
            row = jnp.sum(jnp.where(lane8 == sub8, t, 0.0), axis=0, keepdims=True)
            at = pair * by3 + key
            r["g3"][me[0], me[1], at : at + 1, :] = row
    gather_line(r["g3"], 1, me, count, r["gat"].at[2])
    finish_line(r["c3"], 0, me, count, r["gat"].at[1])
    finish_line(r["g3"], 1, me, count, r["gat"].at[2])
    gather_line(r["g3"], 0, me, count, r["gat"].at[3])

    def assemble(src, dst):
        def body(x, carry):
            for y in range(count[1]):
                for k in range(bx3):
                    dst[x * bx3 + k, y * by3 : (y + 1) * by3, :] = src[
                        x, y, k * by3 : (k + 1) * by3, :
                    ]
            return carry

        lax.fori_loop(0, count[0], body, 0)

    assemble(r["c3"], r["c3w"])
    cond3 = r["c3w"][...]
    w3 = Whole(cond3, 1, 8)
    w4 = Whole(halve(cond3, 8) * 0.25, 2, 16)
    finish_line(r["g3"], 0, me, count, r["gat"].at[3])
    assemble(r["g3"], r["g3w"])
    g3 = r["g3w"][...]
    v3 = w3.ww * g3
    v3 = w3.sweep(v3, g3)
    g4 = halve(g3 + w3.sums(v3) - w3.kk * v3, 8)
    v4 = lax.fori_loop(0, SWEEPS_COARSE - 1, lambda i, v: w4.sweep(v, g4), w4.ww * g4)
    v3 = v3 + double(v4)
    v3 = w3.sweep(v3, g3)
    v3 = w3.sweep(v3, g3)
    r["v3w"][...] = v3

    xmax, ymax = count[0] * bx3 - 1, count[1] * by3 - 1
    for i in range(-1, bx3 + 1):
        x3 = jnp.clip(me[0] * bx3 + i, 0, xmax)
        for j in range(-1, by3 + 1):
            y3 = jnp.clip(me[1] * by3 + j, 0, ymax)
            row = r["v3w"][x3, pl.ds(y3, 1), :]
            t = jnp.where(lane8 == sub8, jnp.broadcast_to(row, (8, l2.nz)), 0.0)
            for step in (1, 2, 4):
                t = pairsum(t, step, 1)
            for dx in (0, 1):
                for dy in (0, 1):
                    x, y = l2.h + 2 * i + dx, l2.h + 2 * j + dy
                    r["p2"][x, y] = r["b2"][x, y] + t
    sweep(l2, co2, r["g2"], r["p2"], r["a2"], 1)
    sweep(l2, co2, r["g2"], r["a2"], r["f2"], 0, shift=l2.h)

    add_correction(l1, r["b1"], r["f2"], r["p1"])
    finish(field_exchange(l1, r["p1"], 6))
    sweep(l1, co1, r["g1"], r["p1"], r["a1"], 1)
    sweep(l1, co1, r["g1"], r["a1"], r["f1"], 0, shift=l1.h)

    add_correction(l0, r["b0"], r["f1"], r["p0"])
    finish(field_exchange(l0, r["p0"], 7))
    sweep(l0, co0, r["g0"], r["p0"], r["a0"], 1)
    sweep(l0, co0, r["g0"], r["a0"], out, 0, shift=l0.h)


def local(count, coil_sources, tissue_labels, class_conductivity):
    _, bx, by, nz = coil_sources.shape
    l0 = Level(0, bx, by, nz, 2, 3)
    l1 = Level(1, bx // 2, by // 2, nz, 2, 3)
    l2 = Level(2, bx // 4, by // 4, nz, 3, 4)
    f32 = jnp.float32
    shapes = {}
    for k, lev in enumerate((l0, l1, l2)):
        for name in ("g", "a", "b", "p"):
            shapes[f"{name}{k}"] = pltpu.VMEM(lev.vshape, f32)
        for name in ("c", "kx", "ky", "kz", "kk", "ww"):
            shapes[f"{name}{k}"] = pltpu.VMEM(lev.cshape, f32)
        if k:
            shapes[f"f{k}"] = pltpu.VMEM((lev.bx, lev.by, 8, nz), f32)
    bx3, by3 = l2.bx // 2, l2.by // 2
    whole = (count[0] * bx3, count[1] * by3, nz)
    for name in ("c3", "g3"):
        shapes[name] = pltpu.VMEM(count + (bx3 * by3, nz), f32)
        shapes[name + "w"] = pltpu.VMEM(whole, f32)
    shapes["v3w"] = pltpu.VMEM(whole, f32)
    shapes["ex"] = pltpu.SemaphoreType.DMA((8, 2, 8))
    shapes["gat"] = pltpu.SemaphoreType.DMA((4, 2, max(count)))
    shapes["local"] = pltpu.SemaphoreType.DMA
    names = list(shapes)

    columns = jnp.transpose(coil_sources, (1, 2, 0, 3))
    result = pl.pallas_call(
        functools.partial(kernel, count, (l0, l1, l2), lambda s: dict(zip(names, s))),
        out_shape=jax.ShapeDtypeStruct(columns.shape, f32),
        in_specs=[
            pl.BlockSpec(memory_space=pltpu.SMEM),
            pl.BlockSpec(memory_space=pl.ANY),
            pl.BlockSpec(memory_space=pltpu.VMEM),
        ],
        out_specs=pl.BlockSpec(memory_space=pltpu.VMEM),
        scratch_shapes=list(shapes.values()),
        compiler_params=pltpu.CompilerParams(
            collective_id=0, has_side_effects=True, vmem_limit_bytes=48 * 2**20
        ),
    )(class_conductivity, columns, tissue_labels)
    return jnp.transpose(result, (2, 0, 1, 3))


def solution(mesh):
    count = (mesh.shape["gx"], mesh.shape["gy"])
    in_specs = (P(None, "gx", "gy", None), P("gx", "gy", None), P())
    out_specs = P(None, "gx", "gy", None)
    return jax.shard_map(
        functools.partial(local, count),
        mesh=mesh,
        in_specs=in_specs,
        out_specs=out_specs,
        check_vma=False,
    )
```

time: 574 us -> 87.4 us (0.15)
  the two profiles are of different devices: /device:TPU:16 before, /device:TPU:1 now
where the time goes in v1:
time: 87.4 us; the launch traced here: 85.8 us
  Pallas kernels  80.8 us (92%)
  local copies, waits for them, and re-layouts  4.98 us (6%)
    pallas_call x1, Pallas kernels, local(): pl.pallas_call(functools.partial(kernel, count, (l0, l1, l2), lambda s: d...  80.8 us
    unnamed x5, local copies, waits for them, and re-layouts  3.28 us

profile of v1, /device:TPU:1, one launch (start us, length us, event | category | flops | bytes accessed | tf_op | source)
XLA Modules:
  0.0 85.8 jit_solution(6292794264499731241)
XLA Ops:
  0.0 0.0 copy-start.1
  0.0 0.0 copy-start
  0.0 3.3 %copy.7 = f32[8,16,32,128]{3,0,2,1:T(8,128)S(1)} copy(f32[8,16,32,128]{3,2,1,0:T(8,128)} %param.3) | data formatting | bytes 4194304 | tf_op args[0]
  3.3 0.0 copy-done.1
  3.3 0.0 copy-done
  3.3 80.8 %shard_map.37 = f32[16,32,8,128]{3,2,1,0:T(8,128)S(1)} custom-call(f32[6]{0:T(128)S(1)} %copy-done.1, f32[16,32,8,128]{3,2,1,0:T(8,128)S(1)} %bitcast.5, s32[16,32,128]{2,1,0:T(8,128)S(1)} %copy-done), custom_call_target="tpu_custom_call" | custom-call | tf_op jit(solution)/shard_map/pallas_call | solution.py:481
  84.1 1.7 %copy.5 = f32[8,16,32,128]{3,2,1,0:T(8,128)} copy(f32[8,16,32,128]{3,0,2,1:T(8,128)S(1)} %bitcast.4) | data formatting | bytes 4194304 | tf_op jit(solution)/shard_map/transpose | solution.py:495
Async XLA Ops:
  0.0 3.3 %copy-start.1 = (f32[6]{0:T(128)S(1)}, f32[6]{0:T(128)}, u32[]{:S(2)}) copy-start(f32[6]{0:T(128)} %table.1) | copy-start | bytes 76
  0.0 3.3 %copy-start = (s32[16,32,128]{2,1,0:T(8,128)S(1)}, s32[16,32,128]{2,1,0:T(8,128)}, u32[]{:S(2)}) copy-start(s32[16,32,128]{2,1,0:T(8,128)} %labels.1) | copy-start | bytes 786436

commit v2 on v1

--- a/solution.py
+++ b/solution.py
@@ -69,14 +69,56 @@
                 device_id_type=MESH,
             )
         )
-    for copy in copies:
-        copy.start()
-    return copies
-
-
-def finish(copies):
-    for copy in copies:
-        copy.wait()
+    pending = []
+    for step, copy in zip(DIRS, copies):
+        to = inside(me, count, step)
+        pl.when(to)(copy.start)
+        pending.append((to, inside(me, count, (-step[0], -step[1])), copy))
+    return pending
+
+
+def inside(me, count, step):
+    there = None
+    for k in (0, 1):
+        if step[k]:
+            ok = me[k] > 0 if step[k] < 0 else me[k] < count[k] - 1
+            there = ok if there is None else jnp.logical_and(there, ok)
+    return there
+
+
+def finish(pending):
+    for to, back, copy in pending:
+        pl.when(to)(copy.wait_send)
+        pl.when(back)(copy.wait_recv)
+
+
+def fill(ref, value):
+    def body(x, carry):
+        ref[x] = jnp.full(ref.shape[1:], value, ref.dtype)
+        return carry
+
+    lax.fori_loop(0, ref.shape[0], body, 0)
+
+
+def clear_halo(lev, ref):
+    zero = jnp.zeros(ref.shape[2:], ref.dtype)
+    ny = ref.shape[1]
+
+    def edge(k, carry):
+        for y in range(ny):
+            ref[k, y] = zero
+            ref[lev.h + lev.bx + k, y] = zero
+        return carry
+
+    lax.fori_loop(0, lev.h, edge, 0)
+
+    def side(x, carry):
+        for k in range(lev.h):
+            ref[x, k] = zero
+            ref[x, lev.h + lev.by + k] = zero
+        return carry
+
+    lax.fori_loop(lev.h, lev.h + lev.bx, side, 0)
 
 
 def coefficients(lev, c, kx, ky, kz, kk, ww, me, count):
@@ -149,9 +191,24 @@
     return (lo, lev.h + lev.bx + width), range(lo, lev.h + lev.by + width)
 
 
-def first_sweep(lev, co, g, out, width):
+def pieces(lev, width, part):
     (x0, x1), ys = spans(lev, width)
-
+    if part == "all":
+        return [(x0, x1, list(ys))]
+    inner = -part[1]
+    (i0, i1), iy = spans(lev, inner)
+    if part[0] == "inner":
+        return [(i0, i1, list(iy))]
+    sides = [y for y in ys if y not in iy]
+    return [(x0, i0, list(ys)), (i1, x1, list(ys)), (i0, i1, sides)]
+
+
+def first_sweep(lev, co, g, out, width, part="all"):
+    for x0, x1, ys in pieces(lev, width, part):
+        first_piece(lev, co, g, out, x0, x1, ys)
+
+
+def first_piece(lev, co, g, out, x0, x1, ys):
     def body(x, carry):
         xc = x + lev.hc - lev.h
         for y in ys:
@@ -162,9 +219,12 @@
     lax.fori_loop(x0, x1, body, 0)
 
 
-def sweep(lev, co, g, v, out, width, shift=0):
-    (x0, x1), ys = spans(lev, width)
-
+def sweep(lev, co, g, v, out, width, shift=0, part="all"):
+    for x0, x1, ys in pieces(lev, width, part):
+        sweep_piece(lev, co, g, v, out, shift, x0, x1, ys)
+
+
+def sweep_piece(lev, co, g, v, out, shift, x0, x1, ys):
     def body(x, carry):
         def emit(y, here, total, at):
             out[x - shift, y - shift] = KEEP * here + at(co[4]) * (g[x, y] + total)
@@ -173,6 +233,14 @@
         return carry
 
     lax.fori_loop(x0, x1, body, 0)
+
+
+def relax_twice(lev, co, g, first, second, pending, width):
+    first_sweep(lev, co, g, first, width, part=("inner", 0))
+    sweep(lev, co, g, first, second, width - 1, part=("inner", 1))
+    finish(pending)
+    first_sweep(lev, co, g, first, width, part=("rim", 0))
+    sweep(lev, co, g, first, second, width - 1, part=("rim", 1))
 
 
 def restrict_rows(lev, co, g, v, pair):
@@ -294,6 +362,12 @@
     l0, l1, l2 = levels
     bx3, by3 = l2.bx // 2, l2.by // 2
 
+    for k, lev in enumerate(levels):
+        fill(r[f"c{k}"], 1.0)
+        clear_halo(lev, r[f"g{k}"])
+        if k < 2:
+            clear_halo(lev, r[f"p{k}"])
+
     barrier = pltpu.get_barrier_semaphore()
     greeted = [(d, 0) for d in range(1, count[0])] + [(0, d) for d in range(1, count[1])]
     greeted += [(dx % count[0], dy % count[1]) for dx, dy in DIRS if dx and dy]
@@ -329,16 +403,15 @@
 
     pl.semaphore_wait(barrier, len(greeted))
     e = r["ex"]
-    exg0 = exchange(
-        g_in, r["g0"], (l0.h,) * 2, (l0.bx, l0.by), (l0.h,) * 2, e.at[0], axes, src_offs=(0, 0)
-    )
-
     def cond_exchange(lev, c, k):
         return exchange(
             c, c, (lev.hc, ROWS), (lev.bx, lev.by), (lev.hc, ROWS), e.at[k], axes
         )
 
     exc0 = cond_exchange(l0, c0, 1)
+    exg0 = exchange(
+        g_in, r["g0"], (l0.h,) * 2, (l0.bx, l0.by), (l0.h,) * 2, e.at[0], axes, src_offs=(0, 0)
+    )
     coarsen(c0, l0.hc, l0.bx, l0.by, 1, put1)
     exc1 = cond_exchange(l1, c1, 2)
     coarsen(c1, l1.hc, l1.bx, l1.by, 2, put2)
@@ -352,10 +425,8 @@
     co2 = [r[n + "2"] for n in ("kx", "ky", "kz", "kk", "ww")]
     coefficients(l0, c0, *co0, me, count)
     fetch.wait()
-    finish(exg0)
-
-    first_sweep(l0, co0, r["g0"], r["a0"], 2)
-    sweep(l0, co0, r["g0"], r["a0"], r["b0"], 1)
+
+    relax_twice(l0, co0, r["g0"], r["a0"], r["b0"], exg0, 2)
 
     def down(lev, co, g, v, nxt, gn):
         def body(pair, carry):
@@ -376,9 +447,7 @@
     finish(exc1)
     finish(exc2)
     coefficients(l1, c1, *co1, me, count)
-    finish(exg1)
-    first_sweep(l1, co1, r["g1"], r["a1"], 2)
-    sweep(l1, co1, r["g1"], r["a1"], r["b1"], 1)
+    relax_twice(l1, co1, r["g1"], r["a1"], r["b1"], exg1, 2)
     down(l1, co1, r["g1"], r["b1"], l2, r["g2"])
 
     exg2 = field_exchange(l2, r["g2"], 5)
@@ -442,13 +511,17 @@
     sweep(l2, co2, r["g2"], r["a2"], r["f2"], 0, shift=l2.h)
 
     add_correction(l1, r["b1"], r["f2"], r["p1"])
-    finish(field_exchange(l1, r["p1"], 6))
-    sweep(l1, co1, r["g1"], r["p1"], r["a1"], 1)
+    exp1 = field_exchange(l1, r["p1"], 6)
+    sweep(l1, co1, r["g1"], r["p1"], r["a1"], 1, part=("inner", 1))
+    finish(exp1)
+    sweep(l1, co1, r["g1"], r["p1"], r["a1"], 1, part=("rim", 1))
     sweep(l1, co1, r["g1"], r["a1"], r["f1"], 0, shift=l1.h)
 
     add_correction(l0, r["b0"], r["f1"], r["p0"])
-    finish(field_exchange(l0, r["p0"], 7))
-    sweep(l0, co0, r["g0"], r["p0"], r["a0"], 1)
+    exp0 = field_exchange(l0, r["p0"], 7)
+    sweep(l0, co0, r["g0"], r["p0"], r["a0"], 1, part=("inner", 1))
+    finish(exp0)
+    sweep(l0, co0, r["g0"], r["p0"], r["a0"], 1, part=("rim", 1))
     sweep(l0, co0, r["g0"], r["a0"], out, 0, shift=l0.h)
 
 

time: 87.4 us -> 76.2 us (0.87)
  Pallas kernels: 80.8 us -> 70.1 us
    pallas_call x1, Pallas kernels: 80.8 us -> 70.1 us  [local(): pl.pallas_call(functools.partial(kernel, count, (l0, l1, l2), lambda s: d...]
where the time goes in v2:
time: 76.2 us; the launch traced here: 75.1 us
  Pallas kernels  70.1 us (92%)
  local copies, waits for them, and re-layouts  4.98 us (7%)
    pallas_call x1, Pallas kernels, local(): pl.pallas_call(functools.partial(kernel, count, (l0, l1, l2), lambda s: d...  70.1 us
    unnamed x5, local copies, waits for them, and re-layouts  3.28 us
    transpose x1, local copies, waits for them, and re-layouts, local(): return jnp.transpose(result, (2, 0, 1, 3))  1.7 us

profile of v2, /device:TPU:1, one launch (start us, length us, event | category | flops | bytes accessed | tf_op | source)
XLA Modules:
  0.0 75.1 jit_solution(9110027543983317097)
XLA Ops:
  0.0 0.0 copy-start.1
  0.0 0.0 copy-start
  0.0 3.3 %copy.7 = f32[8,16,32,128]{3,0,2,1:T(8,128)S(1)} copy(f32[8,16,32,128]{3,2,1,0:T(8,128)} %param.3) | data formatting | bytes 4194304 | tf_op args[0]
  3.3 0.0 copy-done.1
  3.3 0.0 copy-done
  3.3 70.1 %shard_map.37 = f32[16,32,8,128]{3,2,1,0:T(8,128)S(1)} custom-call(f32[6]{0:T(128)S(1)} %copy-done.1, f32[16,32,8,128]{3,2,1,0:T(8,128)S(1)} %bitcast.5, s32[16,32,128]{2,1,0:T(8,128)S(1)} %copy-done), custom_call_target="tpu_custom_call" | custom-call | tf_op jit(solution)/shard_map/pallas_call | solution.py:554
  73.4 1.7 %copy.5 = f32[8,16,32,128]{3,2,1,0:T(8,128)} copy(f32[8,16,32,128]{3,0,2,1:T(8,128)S(1)} %bitcast.4) | data formatting | bytes 4194304 | tf_op jit(solution)/shard_map/transpose | solution.py:568
Async XLA Ops:
  0.0 3.3 %copy-start.1 = (f32[6]{0:T(128)S(1)}, f32[6]{0:T(128)}, u32[]{:S(2)}) copy-start(f32[6]{0:T(128)} %table.1) | copy-start | bytes 76
  0.0 3.3 %copy-start = (s32[16,32,128]{2,1,0:T(8,128)S(1)}, s32[16,32,128]{2,1,0:T(8,128)}, u32[]{:S(2)}) copy-start(s32[16,32,128]{2,1,0:T(8,128)} %labels.1) | copy-start | bytes 786436

commit v3 on v2

--- a/solution.py
+++ b/solution.py
@@ -262,10 +262,30 @@
         for dx in (0, 1):
             x = lev.h + 2 * pair + dx
             for y in range(lev.by):
-                out[x, lev.h + y] = v[x, lev.h + y] + corr[pair, y // 2]
+                out[x, lev.h + y] = v[x, lev.h + y] + corr[1 + pair, 1 + y // 2]
         return carry
 
     lax.fori_loop(0, lev.bx // 2, body, 0)
+
+
+def add_halo(lev, corr, out):
+    nx, ny = lev.bx // 2 + 2, lev.by // 2 + 2
+
+    def grow(x, ys):
+        for y in ys:
+            for dx in (0, 1):
+                for dy in (0, 1):
+                    at = (2 * x + dx, 2 * y + dy)
+                    out[at] = out[at] + corr[x, y]
+
+    grow(0, range(ny))
+    grow(nx - 1, range(ny))
+
+    def body(x, carry):
+        grow(x, (0, ny - 1))
+        return carry
+
+    lax.fori_loop(1, nx - 1, body, 0)
 
 
 def coarsen(src, off, bx, by, step, store):
@@ -367,6 +387,7 @@
         clear_halo(lev, r[f"g{k}"])
         if k < 2:
             clear_halo(lev, r[f"p{k}"])
+            fill(r[f"f{k + 1}"], 0.0)
 
     barrier = pltpu.get_barrier_semaphore()
     greeted = [(d, 0) for d in range(1, count[0])] + [(0, d) for d in range(1, count[1])]
@@ -438,10 +459,15 @@
 
     down(l0, co0, r["g0"], r["b0"], l1, r["g1"])
 
-    def field_exchange(lev, f, k):
-        return exchange(f, f, (lev.h,) * 2, (lev.bx, lev.by), (lev.h,) * 2, e.at[k], axes)
+    def field_exchange(lev, f, k, to=None):
+        to = f if to is None else to
+        return exchange(f, to, (lev.h,) * 2, (lev.bx, lev.by), (lev.h,) * 2, e.at[k], axes)
+
+    def correction_exchange(lev, f, k):
+        return exchange(f, f, (1, 1), (lev.bx, lev.by), (1, 1), e.at[k], axes)
 
     exg1 = field_exchange(l1, r["g1"], 4)
+    exp0 = field_exchange(l0, r["b0"], 7, r["p0"])
     finish_line(r["c3"], 1, me, count, r["gat"].at[0])
     gather_line(r["c3"], 0, me, count, r["gat"].at[1])
     finish(exc1)
@@ -451,6 +477,7 @@
     down(l1, co1, r["g1"], r["b1"], l2, r["g2"])
 
     exg2 = field_exchange(l2, r["g2"], 5)
+    exp1 = field_exchange(l1, r["b1"], 6, r["p1"])
     coefficients(l2, c2, *co2, me, count)
     finish(exg2)
     first_sweep(l2, co2, r["g2"], r["a2"], 3)
@@ -508,19 +535,23 @@
                     x, y = l2.h + 2 * i + dx, l2.h + 2 * j + dy
                     r["p2"][x, y] = r["b2"][x, y] + t
     sweep(l2, co2, r["g2"], r["p2"], r["a2"], 1)
-    sweep(l2, co2, r["g2"], r["a2"], r["f2"], 0, shift=l2.h)
-
+    sweep(l2, co2, r["g2"], r["a2"], r["f2"], 0, shift=l2.h - 1)
+
+    exf2 = correction_exchange(l2, r["f2"], 9)
     add_correction(l1, r["b1"], r["f2"], r["p1"])
-    exp1 = field_exchange(l1, r["p1"], 6)
     sweep(l1, co1, r["g1"], r["p1"], r["a1"], 1, part=("inner", 1))
     finish(exp1)
+    finish(exf2)
+    add_halo(l1, r["f2"], r["p1"])
     sweep(l1, co1, r["g1"], r["p1"], r["a1"], 1, part=("rim", 1))
-    sweep(l1, co1, r["g1"], r["a1"], r["f1"], 0, shift=l1.h)
-
+    sweep(l1, co1, r["g1"], r["a1"], r["f1"], 0, shift=l1.h - 1)
+
+    exf1 = correction_exchange(l1, r["f1"], 8)
     add_correction(l0, r["b0"], r["f1"], r["p0"])
-    exp0 = field_exchange(l0, r["p0"], 7)
     sweep(l0, co0, r["g0"], r["p0"], r["a0"], 1, part=("inner", 1))
     finish(exp0)
+    finish(exf1)
+    add_halo(l0, r["f1"], r["p0"])
     sweep(l0, co0, r["g0"], r["p0"], r["a0"], 1, part=("rim", 1))
     sweep(l0, co0, r["g0"], r["a0"], out, 0, shift=l0.h)
 
@@ -538,14 +569,14 @@
         for name in ("c", "kx", "ky", "kz", "kk", "ww"):
             shapes[f"{name}{k}"] = pltpu.VMEM(lev.cshape, f32)
         if k:
-            shapes[f"f{k}"] = pltpu.VMEM((lev.bx, lev.by, 8, nz), f32)
+            shapes[f"f{k}"] = pltpu.VMEM((lev.bx + 2, lev.by + 2, 8, nz), f32)
     bx3, by3 = l2.bx // 2, l2.by // 2
     whole = (count[0] * bx3, count[1] * by3, nz)
     for name in ("c3", "g3"):
         shapes[name] = pltpu.VMEM(count + (bx3 * by3, nz), f32)
         shapes[name + "w"] = pltpu.VMEM(whole, f32)
     shapes["v3w"] = pltpu.VMEM(whole, f32)
-    shapes["ex"] = pltpu.SemaphoreType.DMA((8, 2, 8))
+    shapes["ex"] = pltpu.SemaphoreType.DMA((10, 2, 8))
     shapes["gat"] = pltpu.SemaphoreType.DMA((4, 2, max(count)))
     shapes["local"] = pltpu.SemaphoreType.DMA
     names = list(shapes)

time: 76.2 us -> 73.9 us (0.970)
  Pallas kernels: 70.1 us -> 68.5 us
    pallas_call x1, Pallas kernels: 70.1 us -> 68.5 us  [local(): pl.pallas_call(functools.partial(kernel, count, (l0, l1, l2), lambda s: d...]
where the time goes in v3:
time: 73.9 us; the launch traced here: 73.5 us
  Pallas kernels  68.5 us (93%)
  local copies, waits for them, and re-layouts  4.98 us (7%)
    pallas_call x1, Pallas kernels, local(): pl.pallas_call(functools.partial(kernel, count, (l0, l1, l2), lambda s: d...  68.5 us
    unnamed x5, local copies, waits for them, and re-layouts  3.28 us
    transpose x1, local copies, waits for them, and re-layouts, local(): return jnp.transpose(result, (2, 0, 1, 3))  1.7 us

profile of v3, /device:TPU:1, one launch (start us, length us, event | category | flops | bytes accessed | tf_op | source)
XLA Modules:
  0.0 73.5 jit_solution(3307829123156933374)
XLA Ops:
  0.0 0.0 copy-start.1
  0.0 0.0 copy-start
  0.0 3.3 %copy.7 = f32[8,16,32,128]{3,0,2,1:T(8,128)S(1)} copy(f32[8,16,32,128]{3,2,1,0:T(8,128)} %param.3) | data formatting | bytes 4194304 | tf_op args[0]
  3.3 0.0 copy-done.1
  3.3 0.0 copy-done
  3.3 68.5 %shard_map.37 = f32[16,32,8,128]{3,2,1,0:T(8,128)S(1)} custom-call(f32[6]{0:T(128)S(1)} %copy-done.1, f32[16,32,8,128]{3,2,1,0:T(8,128)S(1)} %bitcast.5, s32[16,32,128]{2,1,0:T(8,128)S(1)} %copy-done), custom_call_target="tpu_custom_call" | custom-call | tf_op jit(solution)/shard_map/pallas_call | solution.py:585
  71.8 1.7 %copy.5 = f32[8,16,32,128]{3,2,1,0:T(8,128)} copy(f32[8,16,32,128]{3,0,2,1:T(8,128)S(1)} %bitcast.4) | data formatting | bytes 4194304 | tf_op jit(solution)/shard_map/transpose | solution.py:599
Async XLA Ops:
  0.0 3.3 %copy-start.1 = (f32[6]{0:T(128)S(1)}, f32[6]{0:T(128)}, u32[]{:S(2)}) copy-start(f32[6]{0:T(128)} %table.1) | copy-start | bytes 76
  0.0 3.3 %copy-start = (s32[16,32,128]{2,1,0:T(8,128)S(1)}, s32[16,32,128]{2,1,0:T(8,128)}, u32[]{:S(2)}) copy-start(s32[16,32,128]{2,1,0:T(8,128)} %labels.1) | copy-start | bytes 786436

commit v4 on v3

--- a/solution.py
+++ b/solution.py
@@ -467,7 +467,6 @@
         return exchange(f, f, (1, 1), (lev.bx, lev.by), (1, 1), e.at[k], axes)
 
     exg1 = field_exchange(l1, r["g1"], 4)
-    exp0 = field_exchange(l0, r["b0"], 7, r["p0"])
     finish_line(r["c3"], 1, me, count, r["gat"].at[0])
     gather_line(r["c3"], 0, me, count, r["gat"].at[1])
     finish(exc1)
@@ -477,7 +476,6 @@
     down(l1, co1, r["g1"], r["b1"], l2, r["g2"])
 
     exg2 = field_exchange(l2, r["g2"], 5)
-    exp1 = field_exchange(l1, r["b1"], 6, r["p1"])
     coefficients(l2, c2, *co2, me, count)
     finish(exg2)
     first_sweep(l2, co2, r["g2"], r["a2"], 3)
@@ -493,6 +491,8 @@
     finish_line(r["c3"], 0, me, count, r["gat"].at[1])
     finish_line(r["g3"], 1, me, count, r["gat"].at[2])
     gather_line(r["g3"], 0, me, count, r["gat"].at[3])
+    exp1 = field_exchange(l1, r["b1"], 6, r["p1"])
+    exp0 = field_exchange(l0, r["b0"], 7, r["p0"])
 
     def assemble(src, dst):
         def body(x, carry):

time: 73.9 us -> 73 us (0.988)
  no operation moved by 1% of the time
where the time goes in v4:
time: 73 us; the launch traced here: 72.8 us
  Pallas kernels  67.8 us (93%)
  local copies, waits for them, and re-layouts  4.98 us (7%)
    pallas_call x1, Pallas kernels, local(): pl.pallas_call(functools.partial(kernel, count, (l0, l1, l2), lambda s: d...  67.8 us
    unnamed x5, local copies, waits for them, and re-layouts  3.28 us
    transpose x1, local copies, waits for them, and re-layouts, local(): return jnp.transpose(result, (2, 0, 1, 3))  1.7 us

profile of v4, /device:TPU:1, one launch (start us, length us, event | category | flops | bytes accessed | tf_op | source)
XLA Modules:
  0.0 72.8 jit_solution(9868937352476045914)
XLA Ops:
  0.0 0.0 copy-start.1
  0.0 0.0 copy-start
  0.0 3.3 %copy.7 = f32[8,16,32,128]{3,0,2,1:T(8,128)S(1)} copy(f32[8,16,32,128]{3,2,1,0:T(8,128)} %param.3) | data formatting | bytes 4194304 | tf_op args[0]
  3.3 0.0 copy-done.1
  3.3 0.0 copy-done
  3.3 67.8 %shard_map.37 = f32[16,32,8,128]{3,2,1,0:T(8,128)S(1)} custom-call(f32[6]{0:T(128)S(1)} %copy-done.1, f32[16,32,8,128]{3,2,1,0:T(8,128)S(1)} %bitcast.5, s32[16,32,128]{2,1,0:T(8,128)S(1)} %copy-done), custom_call_target="tpu_custom_call" | custom-call | tf_op jit(solution)/shard_map/pallas_call | solution.py:585
  71.2 1.7 %copy.5 = f32[8,16,32,128]{3,2,1,0:T(8,128)} copy(f32[8,16,32,128]{3,0,2,1:T(8,128)S(1)} %bitcast.4) | data formatting | bytes 4194304 | tf_op jit(solution)/shard_map/transpose | solution.py:599
Async XLA Ops:
  0.0 3.3 %copy-start.1 = (f32[6]{0:T(128)S(1)}, f32[6]{0:T(128)}, u32[]{:S(2)}) copy-start(f32[6]{0:T(128)} %table.1) | copy-start | bytes 76
  0.0 3.3 %copy-start = (s32[16,32,128]{2,1,0:T(8,128)S(1)}, s32[16,32,128]{2,1,0:T(8,128)}, u32[]{:S(2)}) copy-start(s32[16,32,128]{2,1,0:T(8,128)} %labels.1) | copy-start | bytes 786436
